TPU v7x, 32 devices: a whole 2x2x4 slice. The times are simulated.
32 devices in a mesh: grp: 2 (over y), sp: 4 (over z), flt: 2 (over x), rep: 2 (over core).
Axes of the slice: x: 2, y: 2, z: 4, core: 2. Of those that a mesh axis runs over, the one named last changes fastest.
Arguments:
- acts: float32 [64, 8, 8, 512], P(None, ('grp', 'sp'), ('flt', 'rep')), parts along dimension 1, may hold values from -6 to 6
- grad_out: float32 [64, 8, 8, 512], P(None, ('grp', 'sp'), ('flt', 'rep')), parts along dimension 1, may hold values from -6 to 6
- kernel: float32 [3, 3, 3, 64, 64], replicated, may hold values from -0.15625 to 0.15625
Outputs:
- input_grad: float32 [64, 8, 8, 512], P(None, ('grp', 'sp'), ('flt', 'rep')), parts along dimension 1
- weight_grad: float32 [6, 3, 3, 64, 64], P('grp'), parts along dimension 0
There are 2 independent parts, one for each index of `grp`. A program takes and returns all parts, laid end to end along the dimension named above; an argument that names none is the same for every part. Nothing has to cross between parts.
All inputs are finite; a program needn't handle non-finite values.
Results may differ from a plain program's by a relative error of at most 0.00007.
Values sent between devices are 32-bit elements; how exact they have to be, the bound alone decides.
A program may use at most 64 MiB of HBM per device.

v0:
```python
import math
import jax
import jax.numpy as jnp
from jax import lax
from jax.sharding import PartitionSpec as P


def padded_2(value, sides, width):
    for axis, dim in sides:
        count, length = (lax.axis_size(axis), value.shape[dim])
        up = [(i, (i + 1) % count) for i in range(count - 1)]
        down = [(j, i) for i, j in up]
        last = lax.slice_in_dim(value, length - width, length, axis=dim)
        first = lax.slice_in_dim(value, 0, width, axis=dim)
        before = lax.ppermute(last, axis, up)
        after = lax.ppermute(first, axis, down)
        value = jnp.concatenate([before, value, after], axis=dim)
    return value


def take_next(values):
    edge = jnp.zeros(values.shape[:-1] + (1,), values.dtype)
    return jnp.concatenate([values[..., 1:], edge], axis=-1)


def take_prior(values):
    edge = jnp.zeros(values.shape[:-1] + (1,), values.dtype)
    return jnp.concatenate([edge, values[..., :-1]], axis=-1)


def contract_last(left, right):
    return lax.dot_general(left, right, (((1,), (1,)), ((), ())), precision=lax.Precision.HIGHEST)


def per_device(acts, grad_out, kernel):
    cin = acts.shape[0]
    planes = acts.shape[1]
    rows = acts.shape[2]
    width = acts.shape[3]
    cout = grad_out.shape[0]
    voxels = (
        planes * lax.axis_size("sp") * rows * lax.axis_size("flt") * lax.axis_size("rep") * width
    )
    factor = 1.0 / math.sqrt(voxels)
    padded = padded_2(grad_out, (("sp", 1), (("flt", "rep"), 2)), 1)
    weights_tap = kernel.reshape(9, 3 * cin, cout)
    weight_terms = [jnp.zeros((3 * cin, cout), jnp.float32) for index in range(9)]
    source = acts[:, 0]
    source_stack = jnp.concatenate([take_prior(source), source, take_next(source)], axis=0).reshape(
        3 * cin, rows * width
    )
    partial_sum = jnp.zeros((3 * cin, rows * width), jnp.float32)
    for a_tap in range(3):
        for b_tap in range(3):
            index = 3 * a_tap + b_tap
            slab = padded[:, 2 - a_tap, 2 - b_tap : 2 - b_tap + rows, :].reshape(cout, rows * width)
            partial_sum = partial_sum + jnp.dot(
                weights_tap[index], slab, precision=lax.Precision.HIGHEST
            )
            weight_terms[index] = contract_last(source_stack, slab)
    parts_x = partial_sum.reshape(3, cin, rows, width)
    plane_out = take_next(parts_x[0]) + parts_x[1] + take_prior(parts_x[2])
    outputs = [plane_out]
    term = jnp.stack(weight_terms, axis=0).reshape(3, 3, 3, cin, cout) * factor
    weight_grad = lax.psum(term, ("sp", "flt", "rep"))
    input_grad = jnp.stack(outputs, axis=1)
    return (input_grad, weight_grad)


def solution(mesh):
    placed = (
        P(None, ("grp", "sp"), ("flt", "rep"), None),
        P(None, ("grp", "sp"), ("flt", "rep"), None),
        P(),
    )
    return jax.shard_map(
        per_device,
        mesh=mesh,
        in_specs=placed,
        out_specs=(P(None, ("grp", "sp"), ("flt", "rep"), None), P("grp", None, None, None, None)),
        check_vma=False,
    )
```

profile of v0, /device:TPU:0, one launch (start us, length us, event | category | flops | bytes accessed | tf_op | source)
XLA Modules:
  0.0 147.4 jit_solution(15860099137105820920)
XLA Ops:
  7.2 1.0 copy.11
  8.2 5.1 %collective-permute-start = (f32[64,1,2,512]{3,0,2,1:T(8,128)S(1)}, f32[64,1,2,512]{3,0,2,1:T(8,128)S(1)}, u32[]{:S(2)}, u32[]{:S(2)}) collective-permute-start(f32[64,1,2,512]{3,0,2,1:T(8,128)S(1)} %copy.11), channel_id=1, source_target_pairs={{0,4},{4,8},{8,12},{1,5},{5,9},{9,13},{2,6},{6,10},{10,14},{3,7},{... | collective-permute-start | bytes 786440 | tf_op jit(solution)/shard_map/ppermute | solution.py:15
  13.3 1.3 collective-permute-start.1
  14.6 4.2 %collective-permute-done = f32[64,1,2,512]{3,0,2,1:T(8,128)S(1)} collective-permute-done((f32[64,1,2,512]{3,0,2,1:T(8,128)S(1)}, f32[64,1,2,512]{3,0,2,1:T(8,128)S(1)}, u32[]{:S(2)}, u32[]{:S(2)}) %collective-permute-start) | collective-permute-done | bytes 262176 | tf_op jit(solution)/shard_map/ppermute | solution.py:15
  18.9 4.0 %collective-permute-done.1 = f32[64,1,2,512]{3,0,2,1:T(8,128)S(1)} collective-permute-done((f32[64,1,2,512]{3,0,2,1:T(8,128)S(1)}, f32[64,1,2,512]{3,0,2,1:T(8,128)S(1)}, u32[]{:S(2)}, u32[]{:S(2)}) %collective-permute-start.1) | collective-permute-done | bytes 262176 | tf_op jit(solution)/shard_map/ppermute | solution.py:16
  23.1 1.3 collective-permute-start.2
  24.4 3.1 %collective-permute-start.3 = (f32[64,3,1,512]{3,0,2,1:T(8,128)S(1)}, f32[64,3,1,512]{3,0,2,1:T(8,128)S(1)}, u32[]{:S(2)}, u32[]{:S(2)}) collective-permute-start(f32[64,3,1,512]{3,0,2,1:T(8,128)S(1)} %get-tuple-element.14), channel_id=1, source_target_pairs={{0,1},{1,2},{2,3},{4,5},{5,6},{6,7},{8,9},{9,10},{10,11},{12,13},{... | collective-permute-start | bytes 1179656 | tf_op jit(solution)/shard_map/ppermute | solution.py:15
  30.9 0.9 fusion.13
  31.7 0.9 fusion.12
  32.6 0.9 fusion.11
  33.5 0.9 fusion.10
  34.4 0.9 fusion.9
  35.2 0.9 fusion.8
  36.1 0.9 fusion.7
  37.0 0.9 fusion.6
  37.9 0.9 fusion.5
  38.8 1.2 copy.22
  40.1 1.1 copy-done.2
  43.5 0.8 fusion.3
  44.3 0.9 convolution_add_fusion.1
  46.0 0.8 fusion.1
  49.4 1.0 add_bitcast_fusion
  50.5 87.9 %all-reduce.6.cloned.1.call-done = f32[3,3,3,64,64]{4,3,2,1,0:T(8,128)} async-done(((f32[3,3,3,64,64]{4,3,2,1,0:T(8,128)}), f32[3,3,3,64,64]{4,3,2,1,0:T(8,128)}) %all-reduce.6.cloned.1.call-update) | async-done | bytes 442384 | tf_op jit(solution)/shard_map/psum | solution.py:65
  138.4 2.2 %copy.49 = f32[3,3,3,64,64]{4,3,2,1,0:T(8,128)} copy(f32[3,3,3,64,64]{4,3,2,1,0:T(8,128)} %all-reduce.6.cloned.1.call-done) | data formatting | bytes 884736
  (52 shorter events, 9.1 us)
Async XLA Ops:
  7.2 131.2 %all-reduce.6.cloned.1.call-start = ((), (), s32[]{:S(2)}) async-start(), calls=%async_computation | async-start | bytes 1769472 | tf_op jit(solution)/shard_map/psum | solution.py:65
  8.2 10.6 %copy-start.1 = (f32[64,1,2,512]{3,2,1,0:T(2,128)S(1)}, f32[64,1,2,512]{3,2,1,0:T(2,128)}, u32[]{:S(2)}) copy-start(f32[64,1,2,512]{3,2,1,0:T(2,128)} %param.4) | copy-start | bytes 786436
  8.2 10.6 %collective-permute-start = (f32[64,1,2,512]{3,0,2,1:T(8,128)S(1)}, f32[64,1,2,512]{3,0,2,1:T(8,128)S(1)}, u32[]{:S(2)}, u32[]{:S(2)}) collective-permute-start(f32[64,1,2,512]{3,0,2,1:T(8,128)S(1)} %copy.11), channel_id=1, source_target_pairs={{0,4},{4,8},{8,12},{1,5},{5,9},{9,13},{2,6},{6,10},{10,14},{3,7},{... | collective-permute-start | bytes 786440 | tf_op jit(solution)/shard_map/ppermute | solution.py:15
  13.3 9.7 %collective-permute-start.1 = (f32[64,1,2,512]{3,0,2,1:T(8,128)S(1)}, f32[64,1,2,512]{3,0,2,1:T(8,128)S(1)}, u32[]{:S(2)}, u32[]{:S(2)}) collective-permute-start(f32[64,1,2,512]{3,0,2,1:T(8,128)S(1)} %copy.11), channel_id=1, source_target_pairs={{4,0},{8,4},{12,8},{5,1},{9,5},{13,9},{6,2},{10,6},{14,10},{7,3},{... | collective-permute-start | bytes 786440 | tf_op jit(solution)/shard_map/ppermute | solution.py:16
  23.0 4.5 %copy-start = (f32[64,1,2,512]{3,2,1,0:T(2,128)S(1)}, f32[64,1,2,512]{3,2,1,0:T(2,128)}, u32[]{:S(2)}) copy-start(f32[64,1,2,512]{3,2,1,0:T(2,128)} %param.3) | copy-start | bytes 786436
  23.1 6.0 %collective-permute-start.2 = (f32[64,3,1,512]{3,0,2,1:T(8,128)S(1)}, f32[64,3,1,512]{3,0,2,1:T(8,128)S(1)}, u32[]{:S(2)}, u32[]{:S(2)}) collective-permute-start(f32[64,3,1,512]{3,0,2,1:T(8,128)S(1)} %get-tuple-element.15), channel_id=1, source_target_pairs={{1,0},{2,1},{3,2},{5,4},{6,5},{7,6},{9,8},{10,9},{11,10},{13,12},{... | collective-permute-start | bytes 1179656 | tf_op jit(solution)/shard_map/ppermute | solution.py:16
  24.4 4.7 %collective-permute-start.3 = (f32[64,3,1,512]{3,0,2,1:T(8,128)S(1)}, f32[64,3,1,512]{3,0,2,1:T(8,128)S(1)}, u32[]{:S(2)}, u32[]{:S(2)}) collective-permute-start(f32[64,3,1,512]{3,0,2,1:T(8,128)S(1)} %get-tuple-element.14), channel_id=1, source_target_pairs={{0,1},{1,2},{2,3},{4,5},{5,6},{6,7},{8,9},{9,10},{10,11},{12,13},{... | collective-permute-start | bytes 1179656 | tf_op jit(solution)/shard_map/ppermute | solution.py:15
  40.0 1.2 copy-start.2
Sparse Core Ops, SparseCore 0:
  40.2 98.1 all-reduce.5
where the time goes:
time: 148 us; the launch traced here: 147 us
  waiting for transfers between devices  96.2 us (65%)
  matrix products  15 us (10%)
  between operations  14.4 us (10%)
  starting transfers between devices  10.8 us (7%)
  local copies, waits for them, and re-layouts  9.81 us (7%)
    psum x1, waiting for transfers between devices, per_device(): weight_grad = lax.psum(term, ('sp', 'flt', 'rep'))  87.9 us
    ppermute x2, starting transfers between devices, padded_2(): before = lax.ppermute(last, axis, up)  8.13 us
    dot_general x9, matrix products, contract_last(): lax.dot_general(left, right, (((1,), (1,)), ((), ())), precision=lax.Prec...  7.91 us
    dot_general x9, matrix products, per_device(): jnp.dot(weights_tap[index], slab, precision=lax.Precision.HIGHEST)  7.09 us
    unnamed x24, local copies, waits for them, and re-layouts  5.03 us
    ppermute x2, waiting for transfers between devices, padded_2(): before = lax.ppermute(last, axis, up)  4.23 us
    ppermute x2, waiting for transfers between devices, padded_2(): after = lax.ppermute(first, axis, down)  4.05 us
  transfers between devices with their start and end apart: 5, of which 3 were waited for; matrix products, arithmetic and copies ran while one was open for 7% of the time, Pallas kernels for 0%

commit v1 on v0

--- a/solution.py
+++ b/solution.py
@@ -62,7 +62,7 @@
     plane_out = take_next(parts_x[0]) + parts_x[1] + take_prior(parts_x[2])
     outputs = [plane_out]
     term = jnp.stack(weight_terms, axis=0).reshape(3, 3, 3, cin, cout) * factor
-    weight_grad = lax.psum(term, ("sp", "flt", "rep"))
+    weight_grad = jnp.sum(lax.all_gather(term, axis_name=("sp", "flt", "rep")), axis=0)
     input_grad = jnp.stack(outputs, axis=1)
     return (input_grad, weight_grad)
 

time: 148 us -> 172 us (1.16)
  waiting for transfers between devices: 96.2 us -> 105 us
  matrix products: 15 us -> 23.1 us
  other arithmetic: 1.21 us -> 9.01 us
  starting transfers between devices: 10.8 us -> 8.88 us
    all_gather x0 -> x1, waiting for transfers between devices: none -> 97.7 us  [per_device(): lax.all_gather(term, axis_name=('sp', 'flt', 'rep'))]
    psum x1 -> x0, waiting for transfers between devices: 87.9 us -> none  [per_device(): weight_grad = lax.psum(term, ('sp', 'flt', 'rep'))]
    dot_general x9, matrix products: 7.09 us -> 15.2 us  [per_device(): jnp.dot(weights_tap[index], slab, precision=lax.Precision.HIGHEST)]
    reduce_sum x0 -> x1, other arithmetic: none -> 7.79 us  [per_device(): jnp.sum(lax.all_gather(term, axis_name=('sp', 'flt', 'rep')), axis=0)]
    ppermute x2, starting transfers between devices: 8.13 us -> 6.26 us  [padded_2(): before = lax.ppermute(last, axis, up)]
    unnamed x24 -> x17, local copies, waits for them, and re-layouts: 5.03 us -> 4.55 us
  transfers between devices with their start and end apart: 5 -> 5, of which waited for: 3 -> 3; matrix products, arithmetic and copies ran while one was open for 7% -> 13% of each run, Pallas kernels for 0% -> 0%
where the time goes in v1:
time: 172 us; the launch traced here: 171 us
  waiting for transfers between devices  105 us (61%)
  matrix products  23.1 us (13%)
  between operations  14.4 us (8%)
  local copies, waits for them, and re-layouts  10.4 us (6%)
  other arithmetic  9.01 us (5%)
  starting transfers between devices  8.88 us (5%)
    all_gather x1, waiting for transfers between devices, per_device(): lax.all_gather(term, axis_name=('sp', 'flt', 'rep'))  97.7 us
    dot_general x9, matrix products, per_device(): jnp.dot(weights_tap[index], slab, precision=lax.Precision.HIGHEST)  15.2 us
    dot_general x9, matrix products, contract_last(): lax.dot_general(left, right, (((1,), (1,)), ((), ())), precision=lax.Prec...  7.91 us
    reduce_sum x1, other arithmetic, per_device(): jnp.sum(lax.all_gather(term, axis_name=('sp', 'flt', 'rep')), axis=0)  7.79 us
    ppermute x2, starting transfers between devices, padded_2(): before = lax.ppermute(last, axis, up)  6.26 us
    unnamed x17, local copies, waits for them, and re-layouts  4.55 us
    ppermute x2, waiting for transfers between devices, padded_2(): before = lax.ppermute(last, axis, up)  4.23 us
  transfers between devices with their start and end apart: 5, of which 3 were waited for; matrix products, arithmetic and copies ran while one was open for 13% of the time, Pallas kernels for 0%

profile of v1, /device:TPU:0, one launch (start us, length us, event | category | flops | bytes accessed | tf_op | source)
XLA Modules:
  0.0 170.9 jit_solution(15440583459284702848)
XLA Ops:
  7.2 1.0 copy.10
  8.2 4.9 %collective-permute-start = (f32[64,1,2,512]{3,0,2,1:T(8,128)S(1)}, f32[64,1,2,512]{3,0,2,1:T(8,128)S(1)}, u32[]{:S(2)}, u32[]{:S(2)}) collective-permute-start(f32[64,1,2,512]{3,0,2,1:T(8,128)S(1)} %copy.10), channel_id=1, source_target_pairs={{0,4},{4,8},{8,12},{1,5},{5,9},{9,13},{2,6},{6,10},{10,14},{3,7},{... | collective-permute-start | bytes 786440 | tf_op jit(solution)/shard_map/ppermute | solution.py:15
  13.2 1.3 collective-permute-start.1
  14.5 4.2 %collective-permute-done = f32[64,1,2,512]{3,0,2,1:T(8,128)S(1)} collective-permute-done((f32[64,1,2,512]{3,0,2,1:T(8,128)S(1)}, f32[64,1,2,512]{3,0,2,1:T(8,128)S(1)}, u32[]{:S(2)}, u32[]{:S(2)}) %collective-permute-start) | collective-permute-done | bytes 262176 | tf_op jit(solution)/shard_map/ppermute | solution.py:15
  18.7 1.0 constant_dynamic-update-slice_fusion.1
  19.7 3.1 %collective-permute-done.1 = f32[64,1,2,512]{3,0,2,1:T(8,128)S(1)} collective-permute-done((f32[64,1,2,512]{3,0,2,1:T(8,128)S(1)}, f32[64,1,2,512]{3,0,2,1:T(8,128)S(1)}, u32[]{:S(2)}, u32[]{:S(2)}) %collective-permute-start.1) | collective-permute-done | bytes 262176 | tf_op jit(solution)/shard_map/ppermute | solution.py:16
  22.9 1.3 collective-permute-start.3
  24.3 1.3 collective-permute-start.2
  25.6 1.4 fusion.16
  26.9 1.0 copy.26
  28.3 1.0 copy.32
  39.8 1.2 copy.21
  41.1 1.7 convolution_bitcast_fusion.5
  42.7 1.7 convolution_add_fusion.2
  44.4 1.7 fusion.4
  46.1 1.7 fusion.3
  47.8 1.8 %convolution_add_fusion.1 = f32[192,1024]{1,0:T(8,128)S(1)} fusion(f32[192,1024]{1,0:T(8,128)S(1)} %fusion.3, f32[64,1024]{1,0:T(8,128)S(1)} %bitcast.167, f32[9,192,64]{2,1,0:T(8,128)} %bitcast.200), kind=kOutput, calls=%fused_computation.7 | convolution fusion | flops 151191552 | bytes 1933312 | tf_op jit(solution)/shard_map/dot_general | solution.py:57
  49.6 1.7 fusion.2
  51.3 1.7 fusion.1
  53.0 1.7 convolution_add_fusion
  54.6 1.7 %fusion = f32[192,1024]{1,0:T(8,128)S(1)} fusion(f32[192,1024]{1,0:T(8,128)S(1)} %convolution_add_fusion, f32[64,1024]{1,0:T(8,128)S(1)} %bitcast.175, f32[9,192,64]{2,1,0:T(8,128)} %bitcast.204), kind=kOutput, calls=%fused_computation.1 | convolution fusion | flops 151191552 | bytes 1933312 | tf_op jit(solution)/shard_map/dot_general | solution.py:57
  57.4 1.0 add_bitcast_fusion
  58.5 97.7 %all-gather.2.cloned.1.call-done = f32[16,3,3,3,64,64]{5,4,3,2,1,0:T(8,128)} async-done(((f32[1,3,3,3,64,64]{5,4,3,2,1,0:T(8,128)}), f32[16,3,3,3,64,64]{5,4,3,2,1,0:T(8,128)}) %all-gather.2.cloned.1.call-update) | async-done | bytes 7077904 | tf_op jit(solution)/shard_map/all_gather | solution.py:65
  156.2 7.8 %reduce_sum.9 = f32[3,3,3,64,64]{4,3,2,1,0:T(8,128)} reduce(f32[16,3,3,3,64,64]{5,4,3,2,1,0:T(8,128)} %all-gather.2.cloned.1.call-done, f32[]{:T(128)} %constant.2.clone.1), dimensions={0}, to_apply=%region_0.0 | reduce | flops 1658880 | bytes 7520260 | tf_op jit(solution)/shard_map/reduce_sum | solution.py:65
  (46 shorter events, 11.9 us)
Async XLA Ops:
  7.2 149.1 %all-gather.2.cloned.1.call-start = ((), (), s32[]{:S(2)}) async-start(), calls=%async_computation | async-start | bytes 15040512 | tf_op jit(solution)/shard_map/all_gather | solution.py:65
  8.2 10.5 %collective-permute-start = (f32[64,1,2,512]{3,0,2,1:T(8,128)S(1)}, f32[64,1,2,512]{3,0,2,1:T(8,128)S(1)}, u32[]{:S(2)}, u32[]{:S(2)}) collective-permute-start(f32[64,1,2,512]{3,0,2,1:T(8,128)S(1)} %copy.10), channel_id=1, source_target_pairs={{0,4},{4,8},{8,12},{1,5},{5,9},{9,13},{2,6},{6,10},{10,14},{3,7},{... | collective-permute-start | bytes 786440 | tf_op jit(solution)/shard_map/ppermute | solution.py:15
  13.2 9.7 %collective-permute-start.1 = (f32[64,1,2,512]{3,0,2,1:T(8,128)S(1)}, f32[64,1,2,512]{3,0,2,1:T(8,128)S(1)}, u32[]{:S(2)}, u32[]{:S(2)}) collective-permute-start(f32[64,1,2,512]{3,0,2,1:T(8,128)S(1)} %copy.10), channel_id=1, source_target_pairs={{4,0},{8,4},{12,8},{5,1},{9,5},{13,9},{6,2},{10,6},{14,10},{7,3},{... | collective-permute-start | bytes 786440 | tf_op jit(solution)/shard_map/ppermute | solution.py:16
  22.9 7.2 %collective-permute-start.3 = (f32[64,3,1,512]{3,0,2,1:T(8,128)S(1)}, f32[64,3,1,512]{3,0,2,1:T(8,128)S(1)}, u32[]{:S(2)}, u32[]{:S(2)}) collective-permute-start(f32[64,3,1,512]{3,0,2,1:T(8,128)S(1)} %get-tuple-element.14), channel_id=1, source_target_pairs={{0,1},{1,2},{2,3},{4,5},{5,6},{6,7},{8,9},{9,10},{10,11},{12,13},{... | collective-permute-start | bytes 1179656 | tf_op jit(solution)/shard_map/ppermute | solution.py:15
  24.3 5.9 %collective-permute-start.2 = (f32[64,3,1,512]{3,0,2,1:T(8,128)S(1)}, f32[64,3,1,512]{3,0,2,1:T(8,128)S(1)}, u32[]{:S(2)}, u32[]{:S(2)}) collective-permute-start(f32[64,3,1,512]{3,0,2,1:T(8,128)S(1)} %get-tuple-element.15), channel_id=1, source_target_pairs={{1,0},{2,1},{3,2},{5,4},{6,5},{7,6},{9,8},{10,9},{11,10},{13,12},{... | collective-permute-start | bytes 1179656 | tf_op jit(solution)/shard_map/ppermute | solution.py:16
Sparse Core Ops, SparseCore 0:
  41.2 114.9 all-gather.1

commit v2 on v0

--- a/solution.py
+++ b/solution.py
@@ -62,7 +62,8 @@
     plane_out = take_next(parts_x[0]) + parts_x[1] + take_prior(parts_x[2])
     outputs = [plane_out]
     term = jnp.stack(weight_terms, axis=0).reshape(3, 3, 3, cin, cout) * factor
-    weight_grad = lax.psum(term, ("sp", "flt", "rep"))
+    one_axis = lax.psum(term, ("flt", "rep"))
+    weight_grad = lax.psum(one_axis, "sp")
     input_grad = jnp.stack(outputs, axis=1)
     return (input_grad, weight_grad)
 

time: 148 us -> 139 us (0.939)
  waiting for transfers between devices: 96.2 us -> 87.8 us
    psum x1 -> x2, waiting for transfers between devices: 87.9 us -> 79.5 us  [the longest x1 47.2 us: per_device(): weight_grad = lax.psum(one_axis, 'sp')]
  transfers between devices with their start and end apart: 5 -> 6, of which waited for: 3 -> 4; matrix products, arithmetic and copies ran while one was open for 7% -> 8% of each run, Pallas kernels for 0% -> 0%
where the time goes in v2:
time: 139 us
  waiting for transfers between devices  87.8 us (63%)
  matrix products  14.9 us (11%)
  between operations  14.4 us (10%)
  starting transfers between devices  11 us (8%)
  local copies, waits for them, and re-layouts  9.59 us (7%)
    psum x1, waiting for transfers between devices, per_device(): weight_grad = lax.psum(one_axis, 'sp')  47.2 us
    psum x1, waiting for transfers between devices, per_device(): one_axis = lax.psum(term, ('flt', 'rep'))  32.3 us
    ppermute x2, starting transfers between devices, padded_2(): before = lax.ppermute(last, axis, up)  8.13 us
    dot_general x9, matrix products, contract_last(): lax.dot_general(left, right, (((1,), (1,)), ((), ())), precision=lax.Prec...  7.91 us
    dot_general x9, matrix products, per_device(): jnp.dot(weights_tap[index], slab, precision=lax.Precision.HIGHEST)  6.98 us
    unnamed x24, local copies, waits for them, and re-layouts  4.8 us
    ppermute x2, waiting for transfers between devices, padded_2(): before = lax.ppermute(last, axis, up)  4.23 us
    ppermute x2, waiting for transfers between devices, padded_2(): after = lax.ppermute(first, axis, down)  4.05 us
  transfers between devices with their start and end apart: 6, of which 4 were waited for; matrix products, arithmetic and copies ran while one was open for 8% of the time, Pallas kernels for 0%

profile of v2, /device:TPU:0, one launch (start us, length us, event | category | flops | bytes accessed | tf_op | source)
XLA Modules:
  0.0 138.9 jit_solution(12874821826051982028)
XLA Ops:
  7.2 1.0 copy.11
  8.2 5.1 %collective-permute-start = (f32[64,1,2,512]{3,0,2,1:T(8,128)S(1)}, f32[64,1,2,512]{3,0,2,1:T(8,128)S(1)}, u32[]{:S(2)}, u32[]{:S(2)}) collective-permute-start(f32[64,1,2,512]{3,0,2,1:T(8,128)S(1)} %copy.11), channel_id=1, source_target_pairs={{0,4},{4,8},{8,12},{1,5},{5,9},{9,13},{2,6},{6,10},{10,14},{3,7},{... | collective-permute-start | bytes 786440 | tf_op jit(solution)/shard_map/ppermute | solution.py:15
  13.3 1.3 collective-permute-start.1
  14.6 4.2 %collective-permute-done = f32[64,1,2,512]{3,0,2,1:T(8,128)S(1)} collective-permute-done((f32[64,1,2,512]{3,0,2,1:T(8,128)S(1)}, f32[64,1,2,512]{3,0,2,1:T(8,128)S(1)}, u32[]{:S(2)}, u32[]{:S(2)}) %collective-permute-start) | collective-permute-done | bytes 262176 | tf_op jit(solution)/shard_map/ppermute | solution.py:15
  18.9 4.0 %collective-permute-done.1 = f32[64,1,2,512]{3,0,2,1:T(8,128)S(1)} collective-permute-done((f32[64,1,2,512]{3,0,2,1:T(8,128)S(1)}, f32[64,1,2,512]{3,0,2,1:T(8,128)S(1)}, u32[]{:S(2)}, u32[]{:S(2)}) %collective-permute-start.1) | collective-permute-done | bytes 262176 | tf_op jit(solution)/shard_map/ppermute | solution.py:16
  23.1 1.3 collective-permute-start.2
  24.4 3.1 %collective-permute-start.3 = (f32[64,3,1,512]{3,0,2,1:T(8,128)S(1)}, f32[64,3,1,512]{3,0,2,1:T(8,128)S(1)}, u32[]{:S(2)}, u32[]{:S(2)}) collective-permute-start(f32[64,3,1,512]{3,0,2,1:T(8,128)S(1)} %get-tuple-element.14), channel_id=1, source_target_pairs={{0,1},{1,2},{2,3},{4,5},{5,6},{6,7},{8,9},{9,10},{10,11},{12,13},{... | collective-permute-start | bytes 1179656 | tf_op jit(solution)/shard_map/ppermute | solution.py:15
  30.9 0.9 fusion.13
  31.7 0.9 fusion.12
  32.6 0.9 fusion.11
  33.5 0.9 fusion.10
  34.4 0.9 fusion.9
  35.2 0.9 fusion.8
  36.1 0.9 fusion.7
  37.0 0.9 fusion.6
  37.9 0.9 fusion.5
  38.8 1.2 copy.22
  40.3 0.9 copy-done.2
  45.9 0.8 fusion.1
  46.7 0.8 convolution_add_fusion
  48.3 32.3 %all-reduce.7.cloned.1.call-done = f32[3,3,3,64,64]{4,3,2,1,0:T(8,128)} async-done(((f32[3,3,3,64,64]{4,3,2,1,0:T(8,128)}), f32[3,3,3,64,64]{4,3,2,1,0:T(8,128)}) %all-reduce.7.cloned.1.call-update) | async-done | bytes 442384 | tf_op jit(solution)/shard_map/psum | solution.py:65
  81.6 1.0 add_bitcast_fusion
  82.7 47.2 %all-reduce.9.cloned.1.call-done = f32[3,3,3,64,64]{4,3,2,1,0:T(8,128)} async-done(((f32[3,3,3,64,64]{4,3,2,1,0:T(8,128)}), f32[3,3,3,64,64]{4,3,2,1,0:T(8,128)}) %all-reduce.9.cloned.1.call-update) | async-done | bytes 442384 | tf_op jit(solution)/shard_map/psum | solution.py:66
  129.9 2.2 %copy.50 = f32[3,3,3,64,64]{4,3,2,1,0:T(8,128)} copy(f32[3,3,3,64,64]{4,3,2,1,0:T(8,128)} %all-reduce.9.cloned.1.call-done) | data formatting | bytes 884736
  (55 shorter events, 10.1 us)
Async XLA Ops:
  7.2 73.4 %all-reduce.7.cloned.1.call-start = ((), (), s32[]{:S(2)}) async-start(), calls=%async_computation | async-start | bytes 1769472 | tf_op jit(solution)/shard_map/psum | solution.py:65
  8.2 10.6 %copy-start.1 = (f32[64,1,2,512]{3,2,1,0:T(2,128)S(1)}, f32[64,1,2,512]{3,2,1,0:T(2,128)}, u32[]{:S(2)}) copy-start(f32[64,1,2,512]{3,2,1,0:T(2,128)} %param.4) | copy-start | bytes 786436
  8.2 10.6 %collective-permute-start = (f32[64,1,2,512]{3,0,2,1:T(8,128)S(1)}, f32[64,1,2,512]{3,0,2,1:T(8,128)S(1)}, u32[]{:S(2)}, u32[]{:S(2)}) collective-permute-start(f32[64,1,2,512]{3,0,2,1:T(8,128)S(1)} %copy.11), channel_id=1, source_target_pairs={{0,4},{4,8},{8,12},{1,5},{5,9},{9,13},{2,6},{6,10},{10,14},{3,7},{... | collective-permute-start | bytes 786440 | tf_op jit(solution)/shard_map/ppermute | solution.py:15
  13.3 9.7 %collective-permute-start.1 = (f32[64,1,2,512]{3,0,2,1:T(8,128)S(1)}, f32[64,1,2,512]{3,0,2,1:T(8,128)S(1)}, u32[]{:S(2)}, u32[]{:S(2)}) collective-permute-start(f32[64,1,2,512]{3,0,2,1:T(8,128)S(1)} %copy.11), channel_id=1, source_target_pairs={{4,0},{8,4},{12,8},{5,1},{9,5},{13,9},{6,2},{10,6},{14,10},{7,3},{... | collective-permute-start | bytes 786440 | tf_op jit(solution)/shard_map/ppermute | solution.py:16
  23.0 4.5 %copy-start = (f32[64,1,2,512]{3,2,1,0:T(2,128)S(1)}, f32[64,1,2,512]{3,2,1,0:T(2,128)}, u32[]{:S(2)}) copy-start(f32[64,1,2,512]{3,2,1,0:T(2,128)} %param.3) | copy-start | bytes 786436
  23.1 6.0 %collective-permute-start.2 = (f32[64,3,1,512]{3,0,2,1:T(8,128)S(1)}, f32[64,3,1,512]{3,0,2,1:T(8,128)S(1)}, u32[]{:S(2)}, u32[]{:S(2)}) collective-permute-start(f32[64,3,1,512]{3,0,2,1:T(8,128)S(1)} %get-tuple-element.15), channel_id=1, source_target_pairs={{1,0},{2,1},{3,2},{5,4},{6,5},{7,6},{9,8},{10,9},{11,10},{13,12},{... | collective-permute-start | bytes 1179656 | tf_op jit(solution)/shard_map/ppermute | solution.py:16
  24.4 4.7 %collective-permute-start.3 = (f32[64,3,1,512]{3,0,2,1:T(8,128)S(1)}, f32[64,3,1,512]{3,0,2,1:T(8,128)S(1)}, u32[]{:S(2)}, u32[]{:S(2)}) collective-permute-start(f32[64,3,1,512]{3,0,2,1:T(8,128)S(1)} %get-tuple-element.14), channel_id=1, source_target_pairs={{0,1},{1,2},{2,3},{4,5},{5,6},{6,7},{8,9},{9,10},{10,11},{12,13},{... | collective-permute-start | bytes 1179656 | tf_op jit(solution)/shard_map/ppermute | solution.py:15
  40.0 1.2 copy-start.2
  40.1 89.8 %all-reduce.9.cloned.1.call-start = ((), (), s32[]{:S(2)}) async-start(), calls=%async_computation.1 | async-start | bytes 1769472 | tf_op jit(solution)/shard_map/psum | solution.py:66
Sparse Core Ops, SparseCore 0:
  40.2 40.3 all-reduce.6
  82.9 46.9 all-reduce.8
